TPU v7x, 128 devices: a whole 4x4x4 slice. The times are simulated.
128 devices in a mesh: frame: 16 (over z_lo, x, core), head: 8 (over z_hi, y).
Axes of the slice: x: 4, y: 4, z: 4 (z_hi: 2, z_lo: 2; z = z_hi * 2 + z_lo), core: 2. Of those that a mesh axis runs over, the one named last changes fastest.
Arguments:
- hidden_in: bfloat16 [10240, 5120], P('frame', 'head'), may hold values from -6 to 6
- queries: bfloat16 [10240, 5120], P('frame', 'head'), may hold values from -90 to 90
- keys: bfloat16 [10240, 5120], P('frame', 'head'), may hold values from -5 to 5
- values: bfloat16 [10240, 5120], P('frame', 'head'), may hold values from -6 to 6
- radial_mask: int32 [16, 6, 5, 5], P('frame'), may hold values from 0 to 1, as said below
- out_weight: bfloat16 [5120, 5120], P('head'), may hold values from -0.078125 to 0.078125
- gate_table: float32 [50, 5120], P(None, 'head'), may hold values from -4 to 4
- timestep: int32 [1], replicated, may hold values from 0 to 49
Outputs:
- layer_out: bfloat16 [10240, 5120], P('frame', 'head')
Inputs may be any that keep to these rules, and one draw needn't show every extreme that they name: `radial_mask`: an entry whose key frame lies outside the video is 0.
All inputs are finite; a program needn't handle non-finite values.
Results may differ from a plain program's by a relative error of at most 0.0055.
Values may be sent and summed in bfloat16 or wider, within the bound.
A program may use at most 192 MiB of HBM per device.

v0:
```python
import jax
import jax.numpy as jnp
from jax import lax
from jax.sharding import PartitionSpec as P

HEAD_DIM = 128
BLK = 128
STEPS = 50


far_offsets = (-8, -4, -2, 2, 4, 8)
neg_large = -1e30


def padded(x, sides, width):
    for axis, dim in sides:
        count, length = (lax.axis_size(axis), x.shape[dim])
        up = [(i, (i + 1) % count) for i in range(count - 1)]
        down = [(j, i) for i, j in up]
        last = lax.slice_in_dim(x, length - width, length, axis=dim)
        first = lax.slice_in_dim(x, 0, width, axis=dim)
        before = lax.ppermute(last, axis, up)
        after = lax.ppermute(first, axis, down)
        x = jnp.concatenate([before, x, after], axis=dim)
    return x


def shifted(block, axis, distance):
    devices = range(lax.axis_size(axis))
    route = [(i - distance, i) for i in devices if i - distance in devices]
    return lax.ppermute(block, axis, route)


def expand_blocks(blocks):
    return jnp.repeat(jnp.repeat(blocks, BLK, axis=0), BLK, axis=1) > 0


def absorb(carry, query_heads, key_rows, value_rows, allowed):
    row_max, row_total, weighted = carry
    head_count = query_heads.shape[1]
    key_heads = key_rows.reshape(key_rows.shape[0], head_count, HEAD_DIM)
    value_heads = value_rows.reshape(value_rows.shape[0], head_count, HEAD_DIM)
    scores = jnp.einsum(
        "qhd,khd->hqk", query_heads, key_heads, preferred_element_type=jnp.float32
    ) * HEAD_DIM ** (-0.5)
    scores = jnp.where(allowed[None], scores, neg_large)
    new_max = jnp.maximum(row_max, jnp.max(scores, axis=-1))
    weights = jnp.where(allowed[None], jnp.exp(scores - new_max[..., None]), 0.0)
    factor = jnp.exp(row_max - new_max)
    new_total = row_total * factor + jnp.sum(weights, axis=-1)
    mixed = jnp.einsum(
        "hqk,khd->hqd",
        weights.astype(jnp.bfloat16),
        value_heads,
        preferred_element_type=jnp.float32,
    )
    return (new_max, new_total, weighted * factor[..., None] + mixed)


def body(hidden_in, queries, keys, values, radial_mask, out_weight, gate_table, timestep):
    tok_rows = queries.shape[0]
    head_count = queries.shape[1] // HEAD_DIM
    block_count = tok_rows // BLK
    query_heads = queries.reshape(tok_rows, head_count, HEAD_DIM)
    my_frame = lax.axis_index("frame")
    frame_total = lax.axis_size("frame")
    carry = (
        jnp.full((head_count, tok_rows), neg_large, jnp.float32),
        jnp.zeros((head_count, tok_rows), jnp.float32),
        jnp.zeros((head_count, tok_rows, HEAD_DIM), jnp.float32),
    )
    key_value = jnp.stack((keys, values))
    banded = padded(key_value, (("frame", 1),), tok_rows)
    previous = banded[:, :tok_rows]
    following = banded[:, 2 * tok_rows :]
    dense_blocks = jnp.ones((block_count, block_count), jnp.int32)
    carry = absorb(carry, query_heads, keys, values, expand_blocks(dense_blocks))
    carry = absorb(
        carry,
        query_heads,
        previous[0],
        previous[1],
        expand_blocks(dense_blocks * (my_frame > 0).astype(jnp.int32)),
    )
    carry = absorb(
        carry,
        query_heads,
        following[0],
        following[1],
        expand_blocks(dense_blocks * (my_frame < frame_total - 1).astype(jnp.int32)),
    )
    for far_slot, distance in enumerate(far_offsets):
        arrived = shifted(key_value, "frame", -distance)
        carry = absorb(
            carry, query_heads, arrived[0], arrived[1], expand_blocks(radial_mask[0, far_slot])
        )
    row_max, row_total, weighted = carry
    attended = (weighted / row_total[..., None]).astype(jnp.bfloat16)
    attended = attended.transpose(1, 0, 2).reshape(tok_rows, head_count * HEAD_DIM)
    term = jnp.dot(attended, out_weight, preferred_element_type=jnp.float32)
    projected = lax.psum_scatter(
        term.astype(jnp.bfloat16), "head", scatter_dimension=1, tiled=True
    ).astype(jnp.float32)
    selector = jnp.arange(STEPS, dtype=jnp.int32)[:, None] == timestep[0]
    gate = jnp.sum(jnp.where(selector, gate_table, 0.0), axis=0)
    return (hidden_in.astype(jnp.float32) + gate[None, :] * projected).astype(jnp.bfloat16)


def solution(mesh):
    in_specs = (
        P("frame", "head"),
        P("frame", "head"),
        P("frame", "head"),
        P("frame", "head"),
        P("frame", None, None, None),
        P("head", None),
        P(None, "head"),
        P(),
    )
    out_specs = P("frame", "head")
    return jax.shard_map(body, mesh=mesh, in_specs=in_specs, out_specs=out_specs, check_vma=False)
```

profile of v0, /device:TPU:32, one launch (start us, length us, event | category | flops | bytes accessed | tf_op | source)
XLA Modules:
  0.0 412.8 jit_solution(17137188508866096970)
XLA Ops:
  6.5 1.8 copy.106
  8.4 1.8 copy.109
  10.2 1.4 pad_maximum_fusion
  12.9 6.9 %collective-permute-start.7 = (bf16[2,640,640]{1,2,0:T(8,128)(2,1)}, bf16[2,640,640]{1,2,0:T(8,128)(2,1)}, u32[]{:S(2)}, u32[]{:S(2)}) collective-permute-start(bf16[2,640,640]{1,2,0:T(8,128)(2,1)} %pad_maximum_fusion), channel_id=1, source_target_pairs={{64,0},{72,8},{80,16},{88,24},{96,32},{104,40},{112,48},{120,56},{... | collective-permute-start | bytes 4915208 | tf_op jit(solution)/shard_map/ppermute | solution.py:31
  19.8 2.5 collective-permute-start.6
  22.4 3.0 collective-permute-start.5
  25.4 1.9 collective-permute-start
  30.5 1.8 copy.105
  32.4 1.5 copy.127
  34.8 2.1 copy.157
  37.7 2.3 copy.151
  40.9 2.3 copy.145
  44.1 2.3 copy.139
  47.3 2.3 copy.133
  51.4 3.3 collective-permute-start.4
  54.7 2.4 fusion.114
  57.2 36.5 %collective-permute-start.3 = (bf16[2,640,640]{1,2,0:T(8,128)(2,1)}, bf16[2,640,640]{1,2,0:T(8,128)(2,1)S(1)}, u32[]{:S(2)}, u32[]{:S(2)}) collective-permute-start(bf16[2,640,640]{1,2,0:T(8,128)(2,1)} %pad_maximum_fusion), channel_id=1, source_target_pairs={{0,32},{8,40},{16,48},{24,56},{32,64},{40,72},{48,80},{56,88},{64,... | collective-permute-start | bytes 4915208 | tf_op jit(solution)/shard_map/ppermute | solution.py:31
  93.7 2.4 fusion.111
  96.2 37.2 %collective-permute-start.1 = (bf16[2,640,640]{1,2,0:T(8,128)(2,1)}, bf16[2,640,640]{1,2,0:T(8,128)(2,1)S(1)}, u32[]{:S(2)}, u32[]{:S(2)}) collective-permute-start(bf16[2,640,640]{1,2,0:T(8,128)(2,1)} %pad_maximum_fusion), channel_id=1, source_target_pairs={{8,0},{16,8},{24,16},{32,24},{40,32},{48,40},{56,48},{64,56},{72,6... | collective-permute-start | bytes 4915208 | tf_op jit(solution)/shard_map/ppermute | solution.py:23
  133.3 2.4 fusion.118
  135.8 2.5 fusion.117
  138.2 2.5 fusion.112
  140.7 4.6 %bitcast_reduce_fusion.1 = (f32[5,640]{1,0:T(8,128)S(1)}, f32[5,640,640]{2,1,0:T(8,128)}) fusion(pred[]{:T(512)S(6)} %gt.121, bf16[640,5,128]{0,2,1:T(8,128)(2,1)S(1)} %bitcast.427, bf16[640,5,128]{0,2,1:T(8,128)(2,1)S(1)} %bitcast.401), kind=kOutput, calls=%fused_computation.11 | convolution fusion | flops 530428800 | bytes 9843201 | tf_op jit(solution)/shard_map/qhd,khd->hqk/dot_general | solution.py:43
  146.3 5.1 %fusion.4 = (f32[5,640]{1,0:T(8,128)S(1)}, f32[5,640,640]{1,2,0:T(8,128)}) fusion(pred[640,640]{1,0:T(8,128)(4,1)S(1)} %copy-done.7, bf16[640,5,128]{0,2,1:T(8,128)(2,1)S(1)} %bitcast.420, bf16[640,5,128]{0,2,1:T(8,128)(2,1)S(1)} %bitcast.402), kind=kOutput, calls=%fused_computation.25 | convolution fusion | flops 530428800 | bytes 10252800 | tf_op jit(solution)/shard_map/qhd,khd->hqk/dot_general | solution.py:43
  151.4 2.1 fusion.9
  153.5 2.0 fusion.8
  156.6 5.1 %fusion.7 = (f32[5,640]{1,0:T(8,128)S(1)}, f32[5,640,640]{1,2,0:T(8,128)}) fusion(pred[640,640]{1,0:T(8,128)(4,1)S(1)} %copy-done.5, bf16[640,5,128]{0,2,1:T(8,128)(2,1)S(1)} %bitcast.422, bf16[640,5,128]{0,2,1:T(8,128)(2,1)S(1)} %bitcast.405), kind=kOutput, calls=%fused_computation.28 | convolution fusion | flops 530428800 | bytes 10252800 | tf_op jit(solution)/shard_map/qhd,khd->hqk/dot_general | solution.py:43
  161.7 16.7 %fusion.6 = (f32[5,640]{1,0:T(8,128)S(1)}, f32[5,640,640]{1,2,0:T(8,128)}) fusion(pred[640,640]{1,0:T(8,128)(4,1)S(1)} %copy-done.9, bf16[640,5,128]{0,2,1:T(8,128)(2,1)S(1)} %bitcast.424, bf16[640,5,128]{0,2,1:T(8,128)(2,1)S(1)} %bitcast.406), kind=kOutput, calls=%fused_computation.27 | convolution fusion | flops 530428800 | bytes 10252800 | tf_op jit(solution)/shard_map/qhd,khd->hqk/dot_general | solution.py:43
  178.4 5.1 %fusion.5 = (f32[5,640]{1,0:T(8,128)S(1)}, f32[5,640,640]{1,2,0:T(8,128)}) fusion(pred[640,640]{1,0:T(8,128)(4,1)S(1)} %copy-done.11, bf16[640,5,128]{0,2,1:T(8,128)(2,1)S(1)} %bitcast.425, bf16[640,5,128]{0,2,1:T(8,128)(2,1)S(1)} %bitcast.407), kind=kOutput, calls=%fused_computation.26 | convolution fusion | flops 530428800 | bytes 10252800 | tf_op jit(solution)/shard_map/qhd,khd->hqk/dot_general | solution.py:43
  184.6 4.5 %bitcast_reduce_fusion = (f32[5,640]{1,0:T(8,128)S(1)}, f32[5,640,640]{2,1,0:T(8,128)}) fusion(pred[]{:T(512)S(6)} %gt.122, bf16[640,5,128]{0,2,1:T(8,128)(2,1)S(1)} %bitcast.426, bf16[640,5,128]{0,2,1:T(8,128)(2,1)S(1)} %bitcast.408), kind=kOutput, calls=%fused_computation.7 | convolution fusion | flops 530428800 | bytes 9843201 | tf_op jit(solution)/shard_map/qhd,khd->hqk/dot_general | solution.py:43
  189.8 2.9 fusion.28
  192.7 3.3 fusion.10
  196.1 3.3 fusion.34
  199.4 5.2 %fusion.26 = f32[5,640]{1,0:T(8,128)S(1)} fusion(f32[5,640,640]{2,1,0:T(8,128)} %get-tuple-element.61, f32[5,640]{1,0:T(8,128)S(1)} %get-tuple-element.21, pred[]{:T(512)S(6)} %gt.122), kind=kLoop, calls=%fused_computation.47 | loop fusion | flops 10236800 | bytes 8217601 | tf_op jit(solution)/shard_map/reduce_sum | solution.py:50
  204.7 6.8 %fusion.32 = f32[5,640,128]{1,2,0:T(8,128)} fusion(bf16[640,5,128]{0,2,1:T(8,128)(2,1)S(1)} %bitcast.441, f32[5,640,640]{2,1,0:T(8,128)} %get-tuple-element.61, f32[5,640]{1,0:T(8,128)S(1)} %get-tuple-element.21, pred[]{:T(512)S(6)} %gt.122), kind=kOutput, calls=%fused_computation.52 | convolution fusion | flops 534528000 | bytes 10662401 | tf_op jit(solution)/shard_map/hqk,khd->hqd/dot_general | solution.py:51
  211.5 4.8 %fusion.46 = f32[5,640,128]{1,2,0:T(8,128)} fusion(bf16[640,5,128]{0,2,1:T(8,128)(2,1)} %bitcast.436, f32[5,640,640]{1,2,0:T(8,128)S(1)} %bitcast.412, f32[5,640]{1,0:T(8,128)S(1)} %get-tuple-element.20, pred[640,640]{1,0:T(8,128)(4,1)S(1)} %copy-done.8), kind=kOutput, calls=%fused_computation.59 | convolution fusion | flops 534528000 | bytes 11072000 | tf_op jit(solution)/shard_map/hqk,khd->hqd/dot_general | solution.py:51
  216.2 7.9 %fusion.12 = (f32[5,640]{1,0:T(8,128)S(1)}, f32[5,640]{1,0:T(8,128)S(1)}) fusion(f32[5,640,640]{1,2,0:T(8,128)S(1)} %bitcast.412, f32[5,640]{1,0:T(8,128)S(1)} %get-tuple-element.20, pred[640,640]{1,0:T(8,128)(4,1)S(1)} %copy-done.8, f32[5,640]{1,0:T(8,128)S(1)} %get-tuple-element.19, f32[5,640,640]{1,2,0:T(8,128)} %get-tuple-element.57, ...), kind=kLoop, calls=%fused_computation.33 | loop fusion | flops 20473600 | bytes 17254400 | tf_op jit(solution)/shard_map/reduce_sum | solution.py:50
  224.1 7.2 %fusion.44 = f32[5,640,128]{1,2,0:T(8,128)} fusion(bf16[640,5,128]{0,2,1:T(8,128)(2,1)} %bitcast.440, f32[5,640,640]{1,2,0:T(8,128)} %get-tuple-element.57, f32[5,640]{1,0:T(8,128)S(1)} %get-tuple-element.19, pred[640,640]{1,0:T(8,128)(4,1)S(1)} %copy-done.12), kind=kOutput, calls=%fused_computation.58 | convolution fusion | flops 534528000 | bytes 11072000 | tf_op jit(solution)/shard_map/hqk,khd->hqd/dot_general | solution.py:51
  231.4 7.3 %fusion.42 = f32[5,640,128]{1,2,0:T(8,128)} fusion(bf16[640,5,128]{0,2,1:T(8,128)(2,1)} %bitcast.438, f32[5,640,640]{1,2,0:T(8,128)} %get-tuple-element.55, f32[5,640]{1,0:T(8,128)S(1)} %get-tuple-element.18, pred[640,640]{1,0:T(8,128)(4,1)S(1)} %copy-done.10), kind=kOutput, calls=%fused_computation.57 | convolution fusion | flops 534528000 | bytes 11072000 | tf_op jit(solution)/shard_map/hqk,khd->hqd/dot_general | solution.py:51
  238.7 7.7 %fusion.16 = (f32[5,640]{1,0:T(8,128)S(1)}, f32[5,640]{1,0:T(8,128)S(1)}) fusion(f32[5,640,640]{1,2,0:T(8,128)} %get-tuple-element.55, f32[5,640]{1,0:T(8,128)S(1)} %get-tuple-element.18, pred[640,640]{1,0:T(8,128)(4,1)S(1)} %copy-done.10, f32[5,640]{1,0:T(8,128)S(1)} %get-tuple-element.17, f32[5,640,640]{1,2,0:T(8,128)S(1)} %bitcast.410, ...), kind=kLoop, calls=%fused_computation.37 | loop fusion | flops 20473600 | bytes 17254400 | tf_op jit(solution)/shard_map/reduce_sum | solution.py:50
  246.3 4.8 %fusion.40 = f32[5,640,128]{1,2,0:T(8,128)} fusion(bf16[640,5,128]{0,2,1:T(8,128)(2,1)} %bitcast.437, f32[5,640,640]{1,2,0:T(8,128)S(1)} %bitcast.410, f32[5,640]{1,0:T(8,128)S(1)} %get-tuple-element.17, pred[640,640]{1,0:T(8,128)(4,1)S(1)} %copy-done.6), kind=kOutput, calls=%fused_computation.56 | convolution fusion | flops 534528000 | bytes 11072000 | tf_op jit(solution)/shard_map/hqk,khd->hqd/dot_general | solution.py:51
  251.1 4.8 %fusion.38 = f32[5,640,128]{1,2,0:T(8,128)} fusion(bf16[640,5,128]{0,2,1:T(8,128)(2,1)} %bitcast.435, f32[5,640,640]{1,2,0:T(8,128)S(1)} %get-tuple-element.51, f32[5,640]{1,0:T(8,128)S(1)} %get-tuple-element.16, pred[640,640]{1,0:T(8,128)(4,1)S(1)} %copy-done.4), kind=kOutput, calls=%fused_computation.55 | convolution fusion | flops 534528000 | bytes 11072000 | tf_op jit(solution)/shard_map/hqk,khd->hqd/dot_general | solution.py:51
  256.0 5.8 %fusion.20 = (f32[5,640]{1,0:T(8,128)S(1)}, f32[5,640]{1,0:T(8,128)S(1)}) fusion(f32[5,640,640]{1,2,0:T(8,128)S(1)} %get-tuple-element.51, f32[5,640]{1,0:T(8,128)S(1)} %get-tuple-element.16, pred[640,640]{1,0:T(8,128)(4,1)S(1)} %copy-done.4, f32[5,640]{1,0:T(8,128)S(1)} %get-tuple-element.15, f32[5,640,640]{1,2,0:T(8,128)S(1)} %get-tuple-element.49, ...), kind=kLoop, calls=%fused_computation.41 | loop fusion | flops 20473600 | bytes 17254400 | tf_op jit(solution)/shard_map/reduce_sum | solution.py:50
  261.9 9.1 %fusion.59 = bf16[640,5,128]{0,2,1:T(8,128)(2,1)S(1)} fusion(f32[5,640,128]{1,2,0:T(8,128)} %fusion.38, f32[5,640,128]{1,2,0:T(8,128)} %fusion.40, f32[5,640,128]{1,2,0:T(8,128)} %fusion.42, f32[5,640,128]{1,2,0:T(8,128)} %fusion.44, f32[5,640,128]{1,2,0:T(8,128)} %fusion.46, f32[5,640,128]{1,2,0:T(8,128)S(1)} %copy-done.24, ...), kind=kOutput, calls=%fused_computation.73 | convolution fusion | flops 542310400 | bytes 23488000 | tf_op jit(solution)/shard_map/hqk,khd->hqd/dot_general | solution.py:51
  271.0 9.2 %convolution_convert_fusion = bf16[640,5120]{1,0:T(8,128)(2,1)} fusion(bf16[640,640]{0,1:T(8,128)(2,1)S(1)} %bitcast.449, bf16[640,5120]{1,0:T(8,128)(2,1)} %param.13), kind=kOutput, calls=%fused_computation.23 | convolution fusion | flops 4197580800 | bytes 13926400 | tf_op jit(solution)/shard_map/dot_general | solution.py:100
  280.2 9.5 %copy.188 = bf16[640,5120]{0,1:T(8,128)(2,1)} copy(bf16[640,5120]{1,0:T(8,128)(2,1)} %convolution_convert_fusion) | data formatting | bytes 13107200
  290.6 111.9 %reduce-scatter.4.cloned.1.call-done = bf16[640,640]{1,0:T(8,128)(2,1)} async-done(((bf16[5120,640]{1,0:T(8,128)(2,1)}), bf16[640,640]{1,0:T(8,128)(2,1)}) %reduce-scatter.4.cloned.1.call-update) | async-done | bytes 819216
  402.5 1.8 copy.189
  (123 shorter events, 16.0 us)
Async XLA Ops:
  6.5 396.0 %reduce-scatter.4.cloned.1.call-start = ((), (), s32[]{:S(2)}) async-start(), calls=%async_computation.1 | async-start | bytes 7372800
  11.6 39.8 %collective-permute-start.2 = (bf16[2,640,640]{1,2,0:T(8,128)(2,1)}, bf16[2,640,640]{1,2,0:T(8,128)(2,1)}, u32[]{:S(2)}, u32[]{:S(2)}) collective-permute-start(bf16[2,640,640]{1,2,0:T(8,128)(2,1)} %pad_maximum_fusion), channel_id=1, source_target_pairs={{0,64},{8,72},{16,80},{24,88},{32,96},{40,104},{48,112},{56,120},{... | collective-permute-start | bytes 4915208 | tf_op jit(solution)/shard_map/ppermute | solution.py:31
  12.9 44.3 %collective-permute-start.7 = (bf16[2,640,640]{1,2,0:T(8,128)(2,1)}, bf16[2,640,640]{1,2,0:T(8,128)(2,1)}, u32[]{:S(2)}, u32[]{:S(2)}) collective-permute-start(bf16[2,640,640]{1,2,0:T(8,128)(2,1)} %pad_maximum_fusion), channel_id=1, source_target_pairs={{64,0},{72,8},{80,16},{88,24},{96,32},{104,40},{112,48},{120,56},{... | collective-permute-start | bytes 4915208 | tf_op jit(solution)/shard_map/ppermute | solution.py:31
  19.8 76.3 %collective-permute-start.6 = (bf16[2,640,640]{1,2,0:T(8,128)(2,1)}, bf16[2,640,640]{1,2,0:T(8,128)(2,1)}, u32[]{:S(2)}, u32[]{:S(2)}) collective-permute-start(bf16[2,640,640]{1,2,0:T(8,128)(2,1)} %pad_maximum_fusion), channel_id=1, source_target_pairs={{32,0},{40,8},{48,16},{56,24},{64,32},{72,40},{80,48},{88,56},{96,... | collective-permute-start | bytes 4915208 | tf_op jit(solution)/shard_map/ppermute | solution.py:31
  22.4 113.4 %collective-permute-start.5 = (bf16[2,640,640]{1,2,0:T(8,128)(2,1)}, bf16[2,640,640]{1,2,0:T(8,128)(2,1)}, u32[]{:S(2)}, u32[]{:S(2)}) collective-permute-start(bf16[2,640,640]{1,2,0:T(8,128)(2,1)} %pad_maximum_fusion), channel_id=1, source_target_pairs={{16,0},{24,8},{32,16},{40,24},{48,32},{56,40},{64,48},{72,56},{80,... | collective-permute-start | bytes 4915208 | tf_op jit(solution)/shard_map/ppermute | solution.py:31
  25.4 112.8 %collective-permute-start = (bf16[2,640,640]{1,2,0:T(8,128)(2,1)}, bf16[2,640,640]{1,2,0:T(8,128)(2,1)}, u32[]{:S(2)}, u32[]{:S(2)}) collective-permute-start(bf16[2,640,640]{1,2,0:T(8,128)(2,1)} %pad_maximum_fusion), channel_id=1, source_target_pairs={{0,8},{8,16},{16,24},{24,32},{32,40},{40,48},{48,56},{56,64},{64,7... | collective-permute-start | bytes 4915208 | tf_op jit(solution)/shard_map/ppermute | solution.py:22
  36.9 114.6 %copy-start.1 = (pred[640,640]{1,0:T(8,128)(4,1)}, pred[640,640]{1,0:T(8,128)(4,1)S(1)}, u32[]{:S(2)}) copy-start(pred[640,640]{1,0:T(8,128)(4,1)S(1)} %copy.157) | copy-start | bytes 1228804
  51.4 93.8 %collective-permute-start.4 = (bf16[2,640,640]{1,2,0:T(8,128)(2,1)}, bf16[2,640,640]{1,2,0:T(8,128)(2,1)S(1)}, u32[]{:S(2)}, u32[]{:S(2)}) collective-permute-start(bf16[2,640,640]{1,2,0:T(8,128)(2,1)} %pad_maximum_fusion), channel_id=1, source_target_pairs={{0,16},{8,24},{16,32},{24,40},{32,48},{40,56},{48,64},{56,72},{64,... | collective-permute-start | bytes 4915208 | tf_op jit(solution)/shard_map/ppermute | solution.py:31
  57.2 98.4 %collective-permute-start.3 = (bf16[2,640,640]{1,2,0:T(8,128)(2,1)}, bf16[2,640,640]{1,2,0:T(8,128)(2,1)S(1)}, u32[]{:S(2)}, u32[]{:S(2)}) collective-permute-start(bf16[2,640,640]{1,2,0:T(8,128)(2,1)} %pad_maximum_fusion), channel_id=1, source_target_pairs={{0,32},{8,40},{16,48},{24,56},{32,64},{40,72},{48,80},{56,88},{64,... | collective-permute-start | bytes 4915208 | tf_op jit(solution)/shard_map/ppermute | solution.py:31
  96.2 87.3 %collective-permute-start.1 = (bf16[2,640,640]{1,2,0:T(8,128)(2,1)}, bf16[2,640,640]{1,2,0:T(8,128)(2,1)S(1)}, u32[]{:S(2)}, u32[]{:S(2)}) collective-permute-start(bf16[2,640,640]{1,2,0:T(8,128)(2,1)} %pad_maximum_fusion), channel_id=1, source_target_pairs={{8,0},{16,8},{24,16},{32,24},{40,32},{48,40},{56,48},{64,56},{72,6... | collective-permute-start | bytes 4915208 | tf_op jit(solution)/shard_map/ppermute | solution.py:23
  138.2 8.1 %copy-start.7 = (pred[640,640]{1,0:T(8,128)(4,1)S(1)}, pred[640,640]{1,0:T(8,128)(4,1)}, u32[]{:S(2)}) copy-start(pred[640,640]{1,0:T(8,128)(4,1)} %copy.127) | copy-start | bytes 1228804
  146.3 7.2 %copy-start.3 = (pred[640,640]{1,0:T(8,128)(4,1)S(1)}, pred[640,640]{1,0:T(8,128)(4,1)}, u32[]{:S(2)}) copy-start(pred[640,640]{1,0:T(8,128)(4,1)} %copy.151) | copy-start | bytes 1228804
  153.5 102.4 %copy-start = (f32[5,640,640]{1,2,0:T(8,128)}, f32[5,640,640]{1,2,0:T(8,128)S(1)}, u32[]{:S(2)}) copy-start(f32[5,640,640]{1,2,0:T(8,128)S(1)} %get-tuple-element.49) | copy-start | bytes 24576004
  153.5 3.1 copy-start.5
  155.5 6.1 %copy-start.9 = (pred[640,640]{1,0:T(8,128)(4,1)S(1)}, pred[640,640]{1,0:T(8,128)(4,1)}, u32[]{:S(2)}) copy-start(pred[640,640]{1,0:T(8,128)(4,1)} %copy.139) | copy-start | bytes 1228804
  156.6 21.7 %copy-start.11 = (pred[640,640]{1,0:T(8,128)(4,1)S(1)}, pred[640,640]{1,0:T(8,128)(4,1)}, u32[]{:S(2)}) copy-start(pred[640,640]{1,0:T(8,128)(4,1)} %copy.133) | copy-start | bytes 1228804
  184.6 8.2 %slice-start.4 = ((s8[8192000]{0:T(1024)(128)(4,1)}), s8[4194304]{0:T(1024)(128)(4,1)S(1)}, s32[]{:S(2)}) async-start(s8[8192000]{0:T(1024)(128)(4,1)} %bitcast.413), calls=%async_computation.6 | async-start | bytes 8388608
  189.8 3.0 slice-start.5
  192.7 3.3 copy-start.16
  196.1 8.6 %copy-start.17 = (bf16[1,640,640]{1,2,0:T(8,128)(2,1)S(1)}, bf16[1,640,640]{1,2,0:T(8,128)(2,1)}, u32[]{:S(2)}) copy-start(bf16[1,640,640]{1,2,0:T(8,128)(2,1)} %get-tuple-element.27) | copy-start | bytes 2457604
  204.6 6.8 %slice-start.2 = ((s8[8192000]{0:T(1024)(128)(4,1)}), s8[4194304]{0:T(1024)(128)(4,1)S(1)}, s32[]{:S(2)}) async-start(s8[8192000]{0:T(1024)(128)(4,1)} %bitcast.411), calls=%async_computation.4 | async-start | bytes 8388608
  204.6 6.8 %copy-start.8 = (pred[640,640]{1,0:T(8,128)(4,1)S(1)}, pred[640,640]{1,0:T(8,128)(4,1)}, u32[]{:S(2)}) copy-start(pred[640,640]{1,0:T(8,128)(4,1)} %copy.127) | copy-start | bytes 1228804
  204.7 6.8 %slice-start.3 = ((s8[8192000]{0:T(1024)(128)(4,1)}), s8[3997696]{0:T(1024)(128)(4,1)S(1)}, s32[]{:S(2)}) async-start(s8[8192000]{0:T(1024)(128)(4,1)} %bitcast.411), calls=%async_computation.5 | async-start | bytes 7995392
  211.5 4.8 %copy-start.12 = (pred[640,640]{1,0:T(8,128)(4,1)S(1)}, pred[640,640]{1,0:T(8,128)(4,1)}, u32[]{:S(2)}) copy-start(pred[640,640]{1,0:T(8,128)(4,1)} %copy.133) | copy-start | bytes 1228804
  224.1 7.2 %copy-start.10 = (pred[640,640]{1,0:T(8,128)(4,1)S(1)}, pred[640,640]{1,0:T(8,128)(4,1)}, u32[]{:S(2)}) copy-start(pred[640,640]{1,0:T(8,128)(4,1)} %copy.139) | copy-start | bytes 1228804
  224.1 14.5 %slice-start = ((s8[8192000]{0:T(1024)(128)(4,1)}), s8[4194304]{0:T(1024)(128)(4,1)S(1)}, s32[]{:S(2)}) async-start(s8[8192000]{0:T(1024)(128)(4,1)} %bitcast.409), calls=%async_computation.2 | async-start | bytes 8388608
  231.4 7.3 %slice-start.1 = ((s8[8192000]{0:T(1024)(128)(4,1)}), s8[3997696]{0:T(1024)(128)(4,1)S(1)}, s32[]{:S(2)}) async-start(s8[8192000]{0:T(1024)(128)(4,1)} %bitcast.409), calls=%async_computation.3 | async-start | bytes 7995392
  231.4 7.3 %copy-start.6 = (pred[640,640]{1,0:T(8,128)(4,1)S(1)}, pred[640,640]{1,0:T(8,128)(4,1)}, u32[]{:S(2)}) copy-start(pred[640,640]{1,0:T(8,128)(4,1)} %copy.145) | copy-start | bytes 1228804
  246.3 4.8 %copy-start.4 = (pred[640,640]{1,0:T(8,128)(4,1)S(1)}, pred[640,640]{1,0:T(8,128)(4,1)}, u32[]{:S(2)}) copy-start(pred[640,640]{1,0:T(8,128)(4,1)} %copy.151) | copy-start | bytes 1228804
  251.1 4.8 %copy-start.2 = (pred[640,640]{1,0:T(8,128)(4,1)S(1)}, pred[640,640]{1,0:T(8,128)(4,1)}, u32[]{:S(2)}) copy-start(pred[640,640]{1,0:T(8,128)(4,1)} %copy-done.1) | copy-start | bytes 1228804
  255.9 5.8 %copy-start.19 = (f32[640,5]{0,1:T(8,128)S(1)}, f32[640,5]{0,1:T(8,128)}, u32[]{:S(2)}) copy-start(f32[640,5]{0,1:T(8,128)} %get-tuple-element.13) | copy-start | bytes 38404
  255.9 5.8 %copy-start.20 = (f32[640,5]{0,1:T(8,128)S(1)}, f32[640,5]{0,1:T(8,128)}, u32[]{:S(2)}) copy-start(f32[640,5]{0,1:T(8,128)} %get-tuple-element.14) | copy-start | bytes 38404
  255.9 5.9 %copy-start.13 = (f32[5,640,128]{1,2,0:T(8,128)S(1)}, f32[5,640,128]{1,2,0:T(8,128)}, u32[]{:S(2)}) copy-start(f32[5,640,128]{1,2,0:T(8,128)} %fusion.28) | copy-start | bytes 4915204
  255.9 5.9 %copy-start.15 = (bf16[1,640,640]{1,2,0:T(8,128)(2,1)S(1)}, bf16[1,640,640]{1,2,0:T(8,128)(2,1)}, u32[]{:S(2)}) copy-start(bf16[1,640,640]{1,2,0:T(8,128)(2,1)} %get-tuple-element.23) | copy-start | bytes 2457604
  256.0 5.9 %copy-start.21 = (f32[640,5]{0,1:T(8,128)S(1)}, f32[640,5]{0,1:T(8,128)}, u32[]{:S(2)}) copy-start(f32[640,5]{0,1:T(8,128)} %get-tuple-element.39) | copy-start | bytes 38404
  256.0 5.9 %copy-start.22 = (f32[640,5]{0,1:T(8,128)S(1)}, f32[640,5]{0,1:T(8,128)}, u32[]{:S(2)}) copy-start(f32[640,5]{0,1:T(8,128)} %get-tuple-element.40) | copy-start | bytes 38404
  256.0 5.9 %copy-start.23 = (f32[5,640,128]{1,2,0:T(8,128)S(1)}, f32[5,640,128]{1,2,0:T(8,128)}, u32[]{:S(2)}) copy-start(f32[5,640,128]{1,2,0:T(8,128)} %fusion.34) | copy-start | bytes 4915204
  256.0 5.9 %copy-start.24 = (f32[5,640,128]{1,2,0:T(8,128)S(1)}, f32[5,640,128]{1,2,0:T(8,128)}, u32[]{:S(2)}) copy-start(f32[5,640,128]{1,2,0:T(8,128)} %fusion.32) | copy-start | bytes 4915204
  280.2 10.2 %copy-start.18 = (f32[50,640]{1,0:T(8,128)S(1)}, f32[50,640]{1,0:T(8,128)}, u32[]{:S(2)}) copy-start(f32[50,640]{1,0:T(8,128)} %param.14) | copy-start | bytes 384004
  280.2 124.1 %copy-start.14 = (bf16[640,640]{1,0:T(8,128)(2,1)S(1)}, bf16[640,640]{1,0:T(8,128)(2,1)}, u32[]{:S(2)}) copy-start(bf16[640,640]{1,0:T(8,128)(2,1)} %param.8) | copy-start | bytes 2457604
Sparse Core Ops, SparseCore 0:
  289.9 112.5 reduce-scatter.3
where the time goes:
time: 421 us; the launch traced here: 413 us
  waiting for transfers between devices  113 us (27%)
  matrix products  107 us (25%)
  starting transfers between devices  92.7 us (22%)
  local copies, waits for them, and re-layouts  52.6 us (12%)
  other arithmetic  33.2 us (8%)
  between operations  15 us (4%)
    unnamed x2, waiting for transfers between devices  112 us
    ppermute x6, starting transfers between devices, shifted(): return lax.ppermute(block, axis, route)  53.6 us
    dot_general x9, matrix products, absorb(): jnp.einsum('hqk,khd->hqd', weights.astype(jnp.bfloat16), value_heads, pre...  51 us
    dot_general x9, matrix products, absorb(): jnp.einsum('qhd,khd->hqk', query_heads, key_heads, preferred_element_type...  46.4 us
    ppermute x1, starting transfers between devices, padded(): after = lax.ppermute(first, axis, down)  37.2 us
    reduce_sum x5, other arithmetic, absorb(): new_total = row_total * factor + jnp.sum(weights, axis=-1)  29.8 us
    unnamed x85, local copies, waits for them, and re-layouts  18.3 us
    gt x12, local copies, waits for them, and re-layouts, expand_blocks(): return jnp.repeat(jnp.repeat(blocks, BLK, axis=0), BLK, axis=1) > 0  13.4 us
  transfers between devices with their start and end apart: 9, of which 2 were waited for; matrix products, arithmetic and copies ran while one was open for 19% of the time, Pallas kernels for 0%

commit v1 on v0

v1 whole, which is shorter than its diff:
```python
import functools

import jax
import jax.numpy as jnp
from jax import lax
from jax.experimental import pallas as pl
from jax.experimental.pallas import tpu as pltpu
from jax.sharding import PartitionSpec as P

MESH = pl.DeviceIdType.MESH
HEAD_DIM = 128
BLK = 128
ROWS = 640
HEADS_LOCAL = 5
GROUPS = 8
SLOTS = 9
OWN, SIB, LEFT, RIGHT, FAR8, FWD, LEFT2, RIGHT2, RELAY = range(9)
SCALE2 = 1.4426950408889634 * HEAD_DIM ** -0.5
NEG = -1e30
HALF = ROWS // 2


def both(*conds):
    out = conds[0]
    for c in conds[1:]:
        out = jnp.logical_and(out, c)
    return out


def kernel(ts_ref, mask_ref, gate_ref, hid_hbm, q_hbm, k_hbm, v_hbm, w_hbm, out_ref,
           kv, qs, att, wcol, hid, bias, m_s, l_s, acc, proj,
           loc, kv_send, kv_recv, at_send, at_recv, w_send, w_recv, ws_send, ws_recv):
    f = lax.axis_index("frame")
    g = lax.axis_index("head")
    core = lax.rem(f, 2)
    sib = f + 1 - 2 * core
    f8 = lax.rem(f + 8, 16)
    zh = g // 4
    y = lax.rem(g, 4)
    other = 1 - zh

    def same(j):
        return zh * 4 + lax.rem(y + j, 4)

    def cross(j):
        return other * 4 + lax.rem(y + j, 4)

    is_a = f < 2
    is_b = both(f >= 6, f < 8)
    is_c = both(f >= 8, f < 10)
    is_d = f >= 14
    not_b = jnp.logical_or(f < 6, f >= 8)
    not_c = jnp.logical_or(f < 8, f >= 10)
    always = f >= 0
    inner = both(f >= 2, f < 14)
    odd = core == 1
    even = core == 0

    local = []
    for h in range(HEADS_LOCAL):
        cols = pl.ds(h * HEAD_DIM, HEAD_DIM)
        local.append([
            pltpu.make_async_copy(k_hbm.at[:, cols], kv.at[OWN, h, 0], loc.at[3 * h]),
            pltpu.make_async_copy(v_hbm.at[:, cols], kv.at[OWN, h, 1], loc.at[3 * h + 1]),
            pltpu.make_async_copy(q_hbm.at[:, cols], qs.at[h], loc.at[3 * h + 2]),
        ])
    for copies in local:
        for c in copies:
            c.start()
    own_cols = pl.ds(pl.multiple_of(g * ROWS, 128), ROWS)
    w_local = pltpu.make_async_copy(w_hbm.at[:, own_cols], wcol.at[g], loc.at[15])
    hid_local = pltpu.make_async_copy(hid_hbm, hid, loc.at[16])

    barrier = pltpu.get_barrier_semaphore()
    peers = [
        (always, (sib, g)), (always, (f8, g)),
        (both(f < 14, not_b), (f + 2, g)), (both(f >= 2, not_c), (f - 2, g)),
        (jnp.logical_or(is_a, is_c), (f + 6, g)), (jnp.logical_or(is_b, is_d), (f - 6, g)),
        (always, (f, cross(0))),
    ]
    peers += [(always, (f, same(j))) for j in (1, 2, 3)]
    peers += [(always, (f8, cross(j))) for j in range(4)]
    count = 0
    for cond, dev in peers:
        if cond is always:
            pl.semaphore_signal(barrier, inc=1, device_id=dev, device_id_type=MESH)
            count = count + 1
        else:
            @pl.when(cond)
            def _(dev=dev):
                pl.semaphore_signal(barrier, inc=1, device_id=dev, device_id_type=MESH)
            count = count + jnp.where(cond, 1, 0)
    pl.semaphore_wait(barrier, count)

    edges = [
        (0, always, OWN, SIB, sib),
        (1, both(f < 14, not_b), OWN, LEFT, f + 2),
        (2, both(f >= 2, not_c), OWN, RIGHT, f - 2),
        (3, always, OWN, FAR8, f8),
        (4, both(inner, not_b), LEFT, LEFT2, f + 2),
        (4, is_b, LEFT, RELAY, f - 6),
        (5, both(inner, not_c), RIGHT, RIGHT2, f - 2),
        (5, is_c, RIGHT, RELAY, f + 6),
        (6, both(odd, f >= 2), LEFT, FWD, f - 1),
        (6, both(even, f < 14), RIGHT, FWD, f + 1),
        (7, is_d, FAR8, LEFT, f - 6),
        (7, is_a, FAR8, RIGHT, f + 6),
        (8, is_a, RELAY, LEFT2, f + 8),
        (8, is_d, RELAY, RIGHT2, f - 8),
    ]

    def kv_copy(h, edge):
        kind, _, src, dst, to = edge
        return pltpu.make_async_remote_copy(
            src_ref=kv.at[src, h], dst_ref=kv.at[dst, h],
            send_sem=kv_send.at[kind, h], recv_sem=kv_recv.at[dst, h],
            device_id=(to, g), device_id_type=MESH)

    def kv_start(h, *kinds):
        for edge in edges:
            if edge[0] in kinds:
                if edge[1] is always:
                    kv_copy(h, edge).start()
                else:
                    @pl.when(edge[1])
                    def _(edge=edge):
                        kv_copy(h, edge).start()

    has = {
        SIB: always, FAR8: always, LEFT: f >= 2, RIGHT: f < 14, LEFT2: f >= 4, RIGHT2: f < 12,
        FWD: jnp.logical_or(both(even, f >= 2), both(odd, f < 14)),
        RELAY: jnp.logical_or(is_a, is_d),
    }

    def kv_wait(h, slot):
        def wait():
            pltpu.make_async_remote_copy(
                src_ref=kv.at[slot, h], dst_ref=kv.at[slot, h],
                send_sem=kv_send.at[0, h], recv_sem=kv_recv.at[slot, h],
                device_id=(sib, g), device_id_type=MESH).wait_recv()
        if has[slot] is always:
            wait()
        else:
            pl.when(has[slot])(wait)

    half = pl.ds(pl.multiple_of(core * HALF, 16), HALF)
    w_peers = [(f, same(j)) for j in (1, 2, 3)] + [(f8, cross(j)) for j in range(4)]

    def w_copy(i):
        frame, group = w_peers[i]
        cols = pl.ds(pl.multiple_of(group * ROWS, 128), ROWS)
        return pltpu.make_async_remote_copy(
            src_ref=w_hbm.at[half, cols], dst_ref=wcol.at[g, half],
            send_sem=w_send.at[i], recv_sem=w_recv.at[g],
            device_id=(frame, group), device_id_type=MESH)

    def w_wait(i):
        group = w_peers[i][1]
        pltpu.make_async_remote_copy(
            src_ref=wcol.at[group, half], dst_ref=wcol.at[group, half],
            send_sem=w_send.at[i], recv_sem=w_recv.at[group],
            device_id=(sib, g), device_id_type=MESH).wait_recv()

    def w_forward(i):
        group = w_peers[i][1]
        return pltpu.make_async_remote_copy(
            src_ref=wcol.at[group, half], dst_ref=wcol.at[group, half],
            send_sem=ws_send.at[i], recv_sem=ws_recv.at[group],
            device_id=(sib, g), device_id_type=MESH)

    def ws_wait(i):
        group = w_peers[i][1]
        theirs = pl.ds(pl.multiple_of((1 - core) * HALF, 16), HALF)
        pltpu.make_async_remote_copy(
            src_ref=wcol.at[group, theirs], dst_ref=wcol.at[group, theirs],
            send_sem=ws_send.at[i], recv_sem=ws_recv.at[group],
            device_id=(sib, g), device_id_type=MESH).wait_recv()

    gathers = [
        (0, g, cross(0)), (1, g, same(1)), (2, g, same(3)),
        (3, cross(0), same(1)), (4, cross(0), same(3)),
        (5, same(3), same(1)), (6, cross(1), same(3)),
    ]

    def at_copy(h, kind):
        _, group, to = gathers[kind]
        return pltpu.make_async_remote_copy(
            src_ref=att.at[group, h], dst_ref=att.at[group, h],
            send_sem=at_send.at[kind, h], recv_sem=at_recv.at[group, h],
            device_id=(f, to), device_id_type=MESH)

    def at_wait(h, group):
        pltpu.make_async_remote_copy(
            src_ref=att.at[group, h], dst_ref=att.at[group, h],
            send_sem=at_send.at[0, h], recv_sem=at_recv.at[group, h],
            device_id=(sib, g), device_id_type=MESH).wait_recv()

    def relay_attended(h):
        at_wait(h, cross(0))
        at_copy(h, 3).start()
        at_copy(h, 4).start()
        at_wait(h, same(3))
        at_copy(h, 5).start()
        at_wait(h, cross(1))
        at_copy(h, 6).start()

    def project(h):
        at_wait(h, same(1))
        at_wait(h, same(2))
        at_wait(h, cross(2))
        at_wait(h, cross(3))
        rows = pl.ds(pl.multiple_of(h * HEAD_DIM, 128), HEAD_DIM)
        lhs = jnp.concatenate([att[i, h] for i in range(GROUPS)], axis=1)
        rhs = jnp.concatenate([wcol[i, rows, :] for i in range(GROUPS)], axis=0)
        proj[...] += jnp.dot(lhs, rhs, preferred_element_type=jnp.float32)

    far_row = {LEFT: 0, RIGHT: 1, FAR8: 2, LEFT2: 3, RIGHT2: 4}

    def attend(h, slot):
        def run():
            s_all = lax.dot_general(
                qs[h], kv[slot, h, 0], (((1,), (1,)), ((), ())),
                preferred_element_type=jnp.float32)
            weights = []
            for b in range(ROWS // BLK):
                rows = slice(b * BLK, (b + 1) * BLK)
                s = s_all[rows]
                if slot in far_row:
                    s = s + bias[far_row[slot], b:b + 1, :]
                top = functools.reduce(
                    jnp.maximum, [s[:, i * 128:(i + 1) * 128] for i in range(5)])
                old = m_s[rows, :]
                new = jnp.maximum(old, jnp.max(top, axis=1, keepdims=True))
                factor = jnp.exp2((old - new) * SCALE2)
                parts = [jnp.exp2((s[:, i * 128:(i + 1) * 128] - new) * SCALE2) for i in range(5)]
                m_s[rows, :] = new
                l_s[rows, :] = l_s[rows, :] * factor + functools.reduce(jnp.add, parts)
                acc[rows, :] = acc[rows, :] * factor
                weights.append(jnp.concatenate([p.astype(jnp.bfloat16) for p in parts], axis=1))
            acc[...] += jnp.dot(
                jnp.concatenate(weights, axis=0), kv[slot, h, 1],
                preferred_element_type=jnp.float32)
        cond = always if slot == OWN else has[slot]
        if cond is always:
            run()
        else:
            pl.when(cond)(run)

    for h in range(2):
        for c in local[h]:
            c.wait()
        kv_start(h, 1, 2, 3, 0)
    w_local.start()
    hid_local.start()
    for i in range(7):
        w_copy(i).start()
    for h in range(2, HEADS_LOCAL):
        for c in local[h]:
            c.wait()

    far8_row = 5 - 5 * (f // 8)
    for slot, source in ((LEFT, 2), (RIGHT, 3), (FAR8, far8_row), (LEFT2, 1), (RIGHT2, 4)):
        for a in range(5):
            for b in range(5):
                value = (mask_ref[0, source, a, b].astype(jnp.float32) - 1.0) * (-NEG)
                bias[far_row[slot], a:a + 1, b * BLK:(b + 1) * BLK] = jnp.full((1, BLK), value, jnp.float32)
    proj[...] = jnp.zeros_like(proj)
    w_local.wait()
    hid_local.wait()

    def phase(h, _):
        @pl.when(both(h >= 1, h < HEADS_LOCAL - 1))
        def _():
            kv_start(h + 1, 1, 2, 3, 0)

        m_s[...] = jnp.full_like(m_s, NEG)
        l_s[...] = jnp.zeros_like(l_s)
        acc[...] = jnp.zeros_like(acc)
        attend(h, OWN)
        kv_wait(h, SIB)
        attend(h, SIB)
        kv_wait(h, FAR8)
        kv_start(h, 7)
        kv_wait(h, LEFT)
        kv_wait(h, RIGHT)
        kv_start(h, 4, 5, 6)
        attend(h, FAR8)
        attend(h, LEFT)
        attend(h, RIGHT)
        kv_wait(h, RELAY)
        kv_start(h, 8)

        @pl.when(h >= 1)
        def _():
            relay_attended(h - 1)

        @pl.when(h == 1)
        def _():
            for i in range(7):
                w_wait(i)
                w_forward(i).start()

        kv_wait(h, FWD)
        attend(h, FWD)

        @pl.when(h == 2)
        def _():
            for i in range(7):
                ws_wait(i)

        @pl.when(h >= 2)
        def _():
            project(h - 2)

        kv_wait(h, LEFT2)
        attend(h, LEFT2)
        kv_wait(h, RIGHT2)
        attend(h, RIGHT2)
        total = jnp.sum(l_s[...], axis=1, keepdims=True)
        att[g, h] = (acc[...] / total).astype(jnp.bfloat16)
        at_copy(h, 0).start()
        at_copy(h, 1).start()
        at_copy(h, 2).start()
        return 0

    lax.fori_loop(0, HEADS_LOCAL, phase, 0)
    relay_attended(HEADS_LOCAL - 1)
    project(HEADS_LOCAL - 2)
    project(HEADS_LOCAL - 1)
    gate = gate_ref[pl.ds(ts_ref[0], 1), :]
    out_ref[...] = (hid[...].astype(jnp.float32) + gate * proj[...]).astype(out_ref.dtype)

    def drain(h, _):
        for edge in edges:
            if edge[1] is always:
                kv_copy(h, edge).wait_send()
            else:
                @pl.when(edge[1])
                def _(edge=edge):
                    kv_copy(h, edge).wait_send()
        for kind in range(len(gathers)):
            at_copy(h, kind).wait_send()
        return 0

    lax.fori_loop(0, HEADS_LOCAL, drain, 0)
    for i in range(7):
        w_copy(i).wait_send()
        w_forward(i).wait_send()


def body(hidden_in, queries, keys, values, radial_mask, out_weight, gate_table, timestep):
    any_spec = pl.BlockSpec(memory_space=pl.ANY)
    dma = pltpu.SemaphoreType.DMA
    return pl.pallas_call(
        kernel,
        out_shape=jax.ShapeDtypeStruct((ROWS, ROWS), jnp.bfloat16),
        in_specs=[
            pl.BlockSpec(memory_space=pltpu.SMEM),
            pl.BlockSpec(memory_space=pltpu.SMEM),
            pl.BlockSpec(memory_space=pltpu.VMEM),
            any_spec, any_spec, any_spec, any_spec, any_spec,
        ],
        out_specs=pl.BlockSpec(memory_space=pltpu.VMEM),
        scratch_shapes=[
            pltpu.VMEM((SLOTS, HEADS_LOCAL, 2, ROWS, HEAD_DIM), jnp.bfloat16),
            pltpu.VMEM((HEADS_LOCAL, ROWS, HEAD_DIM), jnp.bfloat16),
            pltpu.VMEM((GROUPS, HEADS_LOCAL, ROWS, HEAD_DIM), jnp.bfloat16),
            pltpu.VMEM((GROUPS, ROWS, ROWS), jnp.bfloat16),
            pltpu.VMEM((ROWS, ROWS), jnp.bfloat16),
            pltpu.VMEM((5, 5, ROWS), jnp.float32),
            pltpu.VMEM((ROWS, HEAD_DIM), jnp.float32),
            pltpu.VMEM((ROWS, HEAD_DIM), jnp.float32),
            pltpu.VMEM((ROWS, HEAD_DIM), jnp.float32),
            pltpu.VMEM((ROWS, ROWS), jnp.float32),
            dma((17,)),
            dma((9, HEADS_LOCAL)), dma((SLOTS, HEADS_LOCAL)),
            dma((7, HEADS_LOCAL)), dma((GROUPS, HEADS_LOCAL)),
            dma((7,)), dma((GROUPS,)), dma((7,)), dma((GROUPS,)),
        ],
        compiler_params=pltpu.CompilerParams(
            collective_id=0, has_side_effects=True, vmem_limit_bytes=60 * 1024 * 1024),
        cost_estimate=pl.CostEstimate(
            flops=14_000_000_000, bytes_accessed=12_000_000, transcendentals=16_000_000),
    )(timestep, radial_mask, gate_table, hidden_in, queries, keys, values, out_weight)


def solution(mesh):
    in_specs = (
        P("frame", "head"), P("frame", "head"), P("frame", "head"), P("frame", "head"),
        P("frame", None, None, None), P("head", None), P(None, "head"), P(),
    )
    return jax.shard_map(
        body, mesh=mesh, in_specs=in_specs, out_specs=P("frame", "head"), check_vma=False)
```

time: 421 us -> 168 us (0.40); the launches traced: 413 us -> 166 us
  Pallas kernels: 0 us -> 161 us
  waiting for transfers between devices: 113 us -> 0 us
  matrix products: 107 us -> 0 us
  starting transfers between devices: 92.7 us -> 0 us
  local copies, waits for them, and re-layouts: 52.6 us -> 3.55 us
  other arithmetic: 33.2 us -> 0 us
  between operations: 15 us -> 0.66 us
    pallas_call x0 -> x1, Pallas kernels: none -> 161 us  [body(): pl.pallas_call(kernel, out_shape=jax.ShapeDtypeStruct((ROWS, ROWS), jnp.b...]
    unnamed x2 -> x0, waiting for transfers between devices: 112 us -> none
    dot_general x19 -> x0, matrix products: 107 us -> none  [the longest x9 51 us: absorb(): jnp.einsum('hqk,khd->hqd', weights.astype(jnp.bfloat16), value_heads, pre...]
    ppermute x8 -> x0, starting transfers between devices: 92.7 us -> none  [the longest x6 53.6 us: shifted(): return lax.ppermute(block, axis, route)]
    reduce_sum x6 -> x0, other arithmetic: 29.9 us -> none  [the longest x5 29.8 us: absorb(): new_total = row_total * factor + jnp.sum(weights, axis=-1)]
    slice x9 -> x0, local copies, waits for them, and re-layouts: 16.5 us -> none  [the longest x5 9.42 us: body(): arrived[1]]
    unnamed x85 -> x2, local copies, waits for them, and re-layouts: 18.3 us -> 3.55 us
    gt x12 -> x0, local copies, waits for them, and re-layouts: 13.4 us -> none  [expand_blocks(): return jnp.repeat(jnp.repeat(blocks, BLK, axis=0), BLK, axis=1) > 0]
  transfers between devices with their start and end apart: 9 -> 0, of which waited for: 2 -> 0; matrix products, arithmetic and copies ran while one was open for 19% -> 0% of each run, Pallas kernels for 0% -> 0%
where the time goes in v1:
time: 168 us; the launch traced here: 166 us
  Pallas kernels  161 us (96%)
  local copies, waits for them, and re-layouts  3.55 us (2%)
    pallas_call x1, Pallas kernels, body(): pl.pallas_call(kernel, out_shape=jax.ShapeDtypeStruct((ROWS, ROWS), jnp.b...  161 us
    unnamed x2, local copies, waits for them, and re-layouts  3.55 us

profile of v1, /device:TPU:32, one launch (start us, length us, event | category | flops | bytes accessed | tf_op | source)
XLA Modules:
  0.0 165.7 jit_solution(14772208435224801842)
XLA Ops:
  0.7 1.4 copy.9.mask_ref
  2.1 161.5 %shard_map.82 = bf16[640,640]{1,0:T(8,128)(2,1)} custom-call(s32[1]{0:T(128)S(6)} %copy.11.ts_ref, s32[1,6,5,5]{3,2,1,0:T(8,128)} %copy.9.mask_ref, f32[50,640]{1,0:T(8,128)} %gate_ref.1, bf16[640,640]{1,0:T(8,128)(2,1)} %hid_hbm.1, bf16[640,640]{1,0:T(8,128)(2,1)} %q_hbm.1, bf16[640,640]{1,0:T(8,128)(2,1)} %k_hbm.1, bf16[640,640]{1,0:T(8,128)(2,1)} %v_hbm.1, ...), custom_call_target="tpu_custom_call" | custom-call | flops 14000000000 | bytes 12000000 | tf_op jit(solution)/shard_map/pallas_call | solution.py:354
  163.6 2.1 %copy.12 = bf16[640,640]{1,0:T(8,128)(2,1)} copy(bf16[640,640]{1,0:T(8,128)(2,1)} %shard_map.82) | data formatting | bytes 1638400

commit v2 on v1

--- a/solution.py
+++ b/solution.py
@@ -18,6 +18,7 @@
 SCALE2 = 1.4426950408889634 * HEAD_DIM ** -0.5
 NEG = -1e30
 HALF = ROWS // 2
+AHEAD = 2
 
 
 def both(*conds):
@@ -27,8 +28,8 @@
     return out
 
 
-def kernel(ts_ref, mask_ref, gate_ref, hid_hbm, q_hbm, k_hbm, v_hbm, w_hbm, out_ref,
-           kv, qs, att, wcol, hid, bias, m_s, l_s, acc, proj,
+def kernel(ts_ref, mask_hbm, gate_hbm, hid_hbm, q_hbm, k_hbm, v_hbm, w_hbm, out_ref,
+           kv, qs, att, wcol, hid, mask_s, gate_s, bias, m_s, l_s, acc, proj,
            loc, kv_send, kv_recv, at_send, at_recv, w_send, w_recv, ws_send, ws_recv):
     f = lax.axis_index("frame")
     g = lax.axis_index("head")
@@ -70,6 +71,8 @@
     own_cols = pl.ds(pl.multiple_of(g * ROWS, 128), ROWS)
     w_local = pltpu.make_async_copy(w_hbm.at[:, own_cols], wcol.at[g], loc.at[15])
     hid_local = pltpu.make_async_copy(hid_hbm, hid, loc.at[16])
+    mask_local = pltpu.make_async_copy(mask_hbm, mask_s, loc.at[17])
+    gate_local = pltpu.make_async_copy(gate_hbm, gate_s, loc.at[18])
 
     barrier = pltpu.get_barrier_semaphore()
     peers = [
@@ -97,16 +100,18 @@
         (1, both(f < 14, not_b), OWN, LEFT, f + 2),
         (2, both(f >= 2, not_c), OWN, RIGHT, f - 2),
         (3, always, OWN, FAR8, f8),
-        (4, both(inner, not_b), LEFT, LEFT2, f + 2),
-        (4, is_b, LEFT, RELAY, f - 6),
-        (5, both(inner, not_c), RIGHT, RIGHT2, f - 2),
-        (5, is_c, RIGHT, RELAY, f + 6),
+        (4, jnp.logical_or(both(f >= 2, f < 6), both(f >= 8, f < 12)), LEFT, LEFT2, f + 2),
+        (4, is_b, LEFT, RIGHT2, f - 6),
+        (5, jnp.logical_or(both(f >= 4, f < 8), both(f >= 10, f < 14)), RIGHT, RIGHT2, f - 2),
+        (5, is_c, RIGHT, LEFT2, f + 6),
         (6, both(odd, f >= 2), LEFT, FWD, f - 1),
         (6, both(even, f < 14), RIGHT, FWD, f + 1),
         (7, is_d, FAR8, LEFT, f - 6),
         (7, is_a, FAR8, RIGHT, f + 6),
-        (8, is_a, RELAY, LEFT2, f + 8),
-        (8, is_d, RELAY, RIGHT2, f - 8),
+        (7, both(f >= 12, f < 14), FAR8, RELAY, f + 2),
+        (7, both(f >= 2, f < 4), FAR8, RELAY, f - 2),
+        (8, is_a, RELAY, RIGHT2, f + 6),
+        (8, is_d, RELAY, LEFT2, f - 6),
     ]
 
     def kv_copy(h, edge):
@@ -180,13 +185,15 @@
         (0, g, cross(0)), (1, g, same(1)), (2, g, same(3)),
         (3, cross(0), same(1)), (4, cross(0), same(3)),
         (5, same(3), same(1)), (6, cross(1), same(3)),
+        (5, g, same(2)), (6, cross(0), same(2)),
     ]
+    LAST = HEADS_LOCAL - 1
 
     def at_copy(h, kind):
-        _, group, to = gathers[kind]
+        slot, group, to = gathers[kind]
         return pltpu.make_async_remote_copy(
             src_ref=att.at[group, h], dst_ref=att.at[group, h],
-            send_sem=at_send.at[kind, h], recv_sem=at_recv.at[group, h],
+            send_sem=at_send.at[slot, h], recv_sem=at_recv.at[group, h],
             device_id=(f, to), device_id_type=MESH)
 
     def at_wait(h, group):
@@ -195,16 +202,23 @@
             send_sem=at_send.at[0, h], recv_sem=at_recv.at[group, h],
             device_id=(sib, g), device_id_type=MESH).wait_recv()
 
-    def relay_attended(h):
+    def relay_attended(h, last=False):
+        h = jnp.int32(h)
         at_wait(h, cross(0))
         at_copy(h, 3).start()
         at_copy(h, 4).start()
+        if last:
+            at_copy(h, 8).start()
+            at_wait(h, same(3))
+            at_wait(h, cross(1))
+            return
         at_wait(h, same(3))
         at_copy(h, 5).start()
         at_wait(h, cross(1))
         at_copy(h, 6).start()
 
     def project(h):
+        h = jnp.int32(h)
         at_wait(h, same(1))
         at_wait(h, same(2))
         at_wait(h, cross(2))
@@ -246,32 +260,64 @@
         else:
             pl.when(cond)(run)
 
-    for h in range(2):
-        for c in local[h]:
-            c.wait()
-        kv_start(h, 1, 2, 3, 0)
+    for c in local[0]:
+        c.wait()
+    kv_start(0, 3)
+    kv_start(0, 1, 2, 0)
+    for c in local[1]:
+        c.wait()
+    kv_start(1, 3)
+    kv_start(1, 1, 2, 0)
     w_local.start()
     hid_local.start()
+    mask_local.start()
+    gate_local.start()
     for i in range(7):
         w_copy(i).start()
     for h in range(2, HEADS_LOCAL):
         for c in local[h]:
             c.wait()
 
-    far8_row = 5 - 5 * (f // 8)
-    for slot, source in ((LEFT, 2), (RIGHT, 3), (FAR8, far8_row), (LEFT2, 1), (RIGHT2, 4)):
-        for a in range(5):
-            for b in range(5):
-                value = (mask_ref[0, source, a, b].astype(jnp.float32) - 1.0) * (-NEG)
-                bias[far_row[slot], a:a + 1, b * BLK:(b + 1) * BLK] = jnp.full((1, BLK), value, jnp.float32)
+    mask_local.wait()
+    for a in range(5):
+        for b in range(5):
+            blocked = (mask_s[a, b].astype(jnp.float32) - 1.0) * (-NEG)
+            far8 = jnp.where(f < 8, blocked[:, 5:6], blocked[:, 0:1])
+            for slot, column in ((LEFT, blocked[:, 2:3]), (RIGHT, blocked[:, 3:4]), (FAR8, far8),
+                                 (LEFT2, blocked[:, 1:2]), (RIGHT2, blocked[:, 4:5])):
+                bias[far_row[slot], a:a + 1, b * BLK:(b + 1) * BLK] = jnp.broadcast_to(column, (1, BLK))
     proj[...] = jnp.zeros_like(proj)
     w_local.wait()
     hid_local.wait()
-
-    def phase(h, _):
-        @pl.when(both(h >= 1, h < HEADS_LOCAL - 1))
-        def _():
-            kv_start(h + 1, 1, 2, 3, 0)
+    gate_local.wait()
+
+    def relay_far(h):
+        kv_wait(h, FAR8)
+        kv_start(h, 7)
+
+    def relay_near(h):
+        @pl.when(f < 8)
+        def _():
+            kv_wait(h, LEFT)
+            kv_start(h, 4)
+            kv_wait(h, RIGHT)
+            kv_start(h, 5, 6)
+
+        @pl.when(f >= 8)
+        def _():
+            kv_wait(h, RIGHT)
+            kv_start(h, 5)
+            kv_wait(h, LEFT)
+            kv_start(h, 4, 6)
+
+    def step(h, _):
+        @pl.when(h < HEADS_LOCAL - 2)
+        def _():
+            kv_start(h + 2, 1, 2, 0)
+
+        @pl.when(h < HEADS_LOCAL - 3)
+        def _():
+            relay_far(h + 3)
 
         m_s[...] = jnp.full_like(m_s, NEG)
         l_s[...] = jnp.zeros_like(l_s)
@@ -279,38 +325,40 @@
         attend(h, OWN)
         kv_wait(h, SIB)
         attend(h, SIB)
-        kv_wait(h, FAR8)
-        kv_start(h, 7)
-        kv_wait(h, LEFT)
-        kv_wait(h, RIGHT)
-        kv_start(h, 4, 5, 6)
         attend(h, FAR8)
+
+        @pl.when(h < HEADS_LOCAL - 1)
+        def _():
+            kv_wait(h + 1, RELAY)
+            kv_start(h + 1, 8)
+            relay_near(h + 1)
+
         attend(h, LEFT)
         attend(h, RIGHT)
-        kv_wait(h, RELAY)
-        kv_start(h, 8)
+
+        kv_wait(h, FWD)
+        attend(h, FWD)
 
         @pl.when(h >= 1)
         def _():
             relay_attended(h - 1)
 
-        @pl.when(h == 1)
+        @pl.when(h == 2)
         def _():
             for i in range(7):
                 w_wait(i)
                 w_forward(i).start()
 
-        kv_wait(h, FWD)
-        attend(h, FWD)
-
-        @pl.when(h == 2)
+        @pl.when(h == 3)
         def _():
             for i in range(7):
                 ws_wait(i)
-
-        @pl.when(h >= 2)
-        def _():
-            project(h - 2)
+            project(0)
+            project(1)
+
+        @pl.when(h == 4)
+        def _():
+            project(2)
 
         kv_wait(h, LEFT2)
         attend(h, LEFT2)
@@ -321,13 +369,26 @@
         at_copy(h, 0).start()
         at_copy(h, 1).start()
         at_copy(h, 2).start()
+
+        @pl.when(h == LAST)
+        def _():
+            at_copy(h, 7).start()
         return 0
 
-    lax.fori_loop(0, HEADS_LOCAL, phase, 0)
-    relay_attended(HEADS_LOCAL - 1)
-    project(HEADS_LOCAL - 2)
-    project(HEADS_LOCAL - 1)
-    gate = gate_ref[pl.ds(ts_ref[0], 1), :]
+    relay_far(0)
+    kv_start(2, 3)
+    relay_far(1)
+    kv_start(3, 3)
+    relay_near(0)
+    kv_wait(0, RELAY)
+    kv_start(0, 8)
+    relay_far(2)
+    kv_start(4, 3)
+    lax.fori_loop(0, HEADS_LOCAL, step, 0)
+    project(3)
+    relay_attended(LAST, last=True)
+    project(4)
+    gate = gate_s[pl.ds(ts_ref[0], 1), :]
     out_ref[...] = (hid[...].astype(jnp.float32) + gate * proj[...]).astype(out_ref.dtype)
 
     def drain(h, _):
@@ -338,7 +399,7 @@
                 @pl.when(edge[1])
                 def _(edge=edge):
                     kv_copy(h, edge).wait_send()
-        for kind in range(len(gathers)):
+        for kind in range(7):
             at_copy(h, kind).wait_send()
         return 0
 
@@ -356,9 +417,7 @@
         out_shape=jax.ShapeDtypeStruct((ROWS, ROWS), jnp.bfloat16),
         in_specs=[
             pl.BlockSpec(memory_space=pltpu.SMEM),
-            pl.BlockSpec(memory_space=pltpu.SMEM),
-            pl.BlockSpec(memory_space=pltpu.VMEM),
-            any_spec, any_spec, any_spec, any_spec, any_spec,
+            any_spec, any_spec, any_spec, any_spec, any_spec, any_spec, any_spec,
         ],
         out_specs=pl.BlockSpec(memory_space=pltpu.VMEM),
         scratch_shapes=[
@@ -367,12 +426,14 @@
             pltpu.VMEM((GROUPS, HEADS_LOCAL, ROWS, HEAD_DIM), jnp.bfloat16),
             pltpu.VMEM((GROUPS, ROWS, ROWS), jnp.bfloat16),
             pltpu.VMEM((ROWS, ROWS), jnp.bfloat16),
+            pltpu.VMEM((5, 5, 1, 6), jnp.int32),
+            pltpu.VMEM((50, ROWS), jnp.float32),
             pltpu.VMEM((5, 5, ROWS), jnp.float32),
             pltpu.VMEM((ROWS, HEAD_DIM), jnp.float32),
             pltpu.VMEM((ROWS, HEAD_DIM), jnp.float32),
             pltpu.VMEM((ROWS, HEAD_DIM), jnp.float32),
             pltpu.VMEM((ROWS, ROWS), jnp.float32),
-            dma((17,)),
+            dma((19,)),
             dma((9, HEADS_LOCAL)), dma((SLOTS, HEADS_LOCAL)),
             dma((7, HEADS_LOCAL)), dma((GROUPS, HEADS_LOCAL)),
             dma((7,)), dma((GROUPS,)), dma((7,)), dma((GROUPS,)),
@@ -381,7 +442,7 @@
             collective_id=0, has_side_effects=True, vmem_limit_bytes=60 * 1024 * 1024),
         cost_estimate=pl.CostEstimate(
             flops=14_000_000_000, bytes_accessed=12_000_000, transcendentals=16_000_000),
-    )(timestep, radial_mask, gate_table, hidden_in, queries, keys, values, out_weight)
+    )(timestep, radial_mask.transpose(2, 3, 0, 1), gate_table, hidden_in, queries, keys, values, out_weight)
 
 
 def solution(mesh):

time: 168 us -> 136 us (0.81); the launches traced: 166 us -> 136 us
  Pallas kernels: 161 us -> 133 us
    pallas_call x1, Pallas kernels: 161 us -> 133 us  [body(): pl.pallas_call(kernel, out_shape=jax.ShapeDtypeStruct((ROWS, ROWS), jnp.b...]
    unnamed x2 -> x1, local copies, waits for them, and re-layouts: 3.55 us -> 2.11 us
where the time goes in v2:
time: 136 us
  Pallas kernels  133 us (98%)
  local copies, waits for them, and re-layouts  2.11 us (2%)
    pallas_call x1, Pallas kernels, body(): pl.pallas_call(kernel, out_shape=jax.ShapeDtypeStruct((ROWS, ROWS), jnp.b...  133 us

profile of v2, /device:TPU:32, one launch (start us, length us, event | category | flops | bytes accessed | tf_op | source)
XLA Modules:
  0.0 136.0 jit_solution(4928267190280874156)
XLA Ops:
  0.7 133.2 %shard_map.82 = bf16[640,640]{1,0:T(8,128)(2,1)} custom-call(s32[1]{0:T(128)S(6)} %copy.10.ts_ref, s32[5,5,1,6]{3,2,1,0:T(1,128)} %bitcast.1, f32[50,640]{1,0:T(8,128)} %gate_hbm.1, bf16[640,640]{1,0:T(8,128)(2,1)} %hid_hbm.1, bf16[640,640]{1,0:T(8,128)(2,1)} %q_hbm.1, bf16[640,640]{1,0:T(8,128)(2,1)} %k_hbm.1, bf16[640,640]{1,0:T(8,128)(2,1)} %v_hbm.1, ...), custom_call_target="tpu_custom_call" | custom-call | flops 14000000000 | bytes 12000000 | tf_op jit(solution)/shard_map/pallas_call | solution.py:415
  133.8 2.1 %copy.11 = bf16[640,640]{1,0:T(8,128)(2,1)} copy(bf16[640,640]{1,0:T(8,128)(2,1)} %shard_map.82) | data formatting | bytes 1638400

commit v3 on v2

--- a/solution.py
+++ b/solution.py
@@ -17,8 +17,8 @@
 OWN, SIB, LEFT, RIGHT, FAR8, FWD, LEFT2, RIGHT2, RELAY = range(9)
 SCALE2 = 1.4426950408889634 * HEAD_DIM ** -0.5
 NEG = -1e30
-HALF = ROWS // 2
-AHEAD = 2
+QUARTER = ROWS // 4
+PASSED = ((0, 2), (1, 3), (4, 6), (5,))
 
 
 def both(*conds):
@@ -37,6 +37,7 @@
     sib = f + 1 - 2 * core
     f8 = lax.rem(f + 8, 16)
     zh = g // 4
+    zl = f // 8
     y = lax.rem(g, 4)
     other = 1 - zh
 
@@ -53,6 +54,7 @@
     not_b = jnp.logical_or(f < 6, f >= 8)
     not_c = jnp.logical_or(f < 8, f >= 10)
     always = f >= 0
+    middle = both(f >= 6, f < 10)
     inner = both(f >= 2, f < 14)
     odd = core == 1
     even = core == 0
@@ -148,37 +150,40 @@
         else:
             pl.when(has[slot])(wait)
 
-    half = pl.ds(pl.multiple_of(core * HALF, 16), HALF)
-    w_peers = [(f, same(j)) for j in (1, 2, 3)] + [(f8, cross(j)) for j in range(4)]
+    def quarter(on_core, on_zl):
+        return pl.ds(pl.multiple_of((on_core * 2 + on_zl) * QUARTER, 16), QUARTER)
+
+    w_peers = [(f, same(j), zl) for j in (1, 2, 3)] + [(f8, cross(j), 1 - zl) for j in range(4)]
 
     def w_copy(i):
-        frame, group = w_peers[i]
+        frame, group, their_zl = w_peers[i]
         cols = pl.ds(pl.multiple_of(group * ROWS, 128), ROWS)
+        rows = quarter(core, their_zl)
         return pltpu.make_async_remote_copy(
-            src_ref=w_hbm.at[half, cols], dst_ref=wcol.at[g, half],
+            src_ref=w_hbm.at[rows, cols], dst_ref=wcol.at[g, rows],
             send_sem=w_send.at[i], recv_sem=w_recv.at[g],
             device_id=(frame, group), device_id_type=MESH)
 
+    def w_pass(i, kind):
+        group = w_peers[i][1]
+        rows = quarter(core, zl if kind < 2 else 1 - zl)
+        return pltpu.make_async_remote_copy(
+            src_ref=wcol.at[group, rows], dst_ref=wcol.at[group, rows],
+            send_sem=ws_send.at[kind, i], recv_sem=ws_recv.at[kind, group],
+            device_id=(f8 if kind == 1 else sib, g), device_id_type=MESH)
+
     def w_wait(i):
         group = w_peers[i][1]
+        ref = wcol.at[group, quarter(core, zl)]
         pltpu.make_async_remote_copy(
-            src_ref=wcol.at[group, half], dst_ref=wcol.at[group, half],
-            send_sem=w_send.at[i], recv_sem=w_recv.at[group],
+            src_ref=ref, dst_ref=ref, send_sem=w_send.at[i], recv_sem=w_recv.at[group],
             device_id=(sib, g), device_id_type=MESH).wait_recv()
 
-    def w_forward(i):
+    def ws_wait(i, kind):
         group = w_peers[i][1]
-        return pltpu.make_async_remote_copy(
-            src_ref=wcol.at[group, half], dst_ref=wcol.at[group, half],
-            send_sem=ws_send.at[i], recv_sem=ws_recv.at[group],
-            device_id=(sib, g), device_id_type=MESH)
-
-    def ws_wait(i):
-        group = w_peers[i][1]
-        theirs = pl.ds(pl.multiple_of((1 - core) * HALF, 16), HALF)
+        ref = wcol.at[group, quarter(core if kind == 1 else 1 - core, zl if kind == 0 else 1 - zl)]
         pltpu.make_async_remote_copy(
-            src_ref=wcol.at[group, theirs], dst_ref=wcol.at[group, theirs],
-            send_sem=ws_send.at[i], recv_sem=ws_recv.at[group],
+            src_ref=ref, dst_ref=ref, send_sem=ws_send.at[kind, i], recv_sem=ws_recv.at[kind, group],
             device_id=(sib, g), device_id_type=MESH).wait_recv()
 
     gathers = [
@@ -188,6 +193,7 @@
         (5, g, same(2)), (6, cross(0), same(2)),
     ]
     LAST = HEADS_LOCAL - 1
+    DIRECT = HEADS_LOCAL - 1
 
     def at_copy(h, kind):
         slot, group, to = gathers[kind]
@@ -202,31 +208,51 @@
             send_sem=at_send.at[0, h], recv_sem=at_recv.at[group, h],
             device_id=(sib, g), device_id_type=MESH).wait_recv()
 
-    def relay_attended(h, last=False):
+    def relay_partner(h):
         h = jnp.int32(h)
         at_wait(h, cross(0))
         at_copy(h, 3).start()
         at_copy(h, 4).start()
-        if last:
+
+        @pl.when(h >= DIRECT)
+        def _():
             at_copy(h, 8).start()
-            at_wait(h, same(3))
-            at_wait(h, cross(1))
-            return
+
+    def relay_same(h):
+        h = jnp.int32(h)
         at_wait(h, same(3))
         at_copy(h, 5).start()
+
+    def relay_cross(h):
+        h = jnp.int32(h)
         at_wait(h, cross(1))
         at_copy(h, 6).start()
 
+    def add_projected(h, groups):
+        rows = pl.ds(pl.multiple_of(h * HEAD_DIM, 128), HEAD_DIM)
+        lhs = jnp.concatenate([att[i, h] for i in groups], axis=1)
+        rhs = jnp.concatenate([wcol[i, rows, :] for i in groups], axis=0)
+        proj[...] += jnp.dot(lhs, rhs, preferred_element_type=jnp.float32)
+
     def project(h):
+        if h >= DIRECT:
+            at_wait(jnp.int32(h), same(3))
+            at_wait(jnp.int32(h), cross(1))
         h = jnp.int32(h)
         at_wait(h, same(1))
         at_wait(h, same(2))
         at_wait(h, cross(2))
         at_wait(h, cross(3))
-        rows = pl.ds(pl.multiple_of(h * HEAD_DIM, 128), HEAD_DIM)
-        lhs = jnp.concatenate([att[i, h] for i in range(GROUPS)], axis=1)
-        rhs = jnp.concatenate([wcol[i, rows, :] for i in range(GROUPS)], axis=0)
-        proj[...] += jnp.dot(lhs, rhs, preferred_element_type=jnp.float32)
+        add_projected(h, range(GROUPS))
+
+    def project_last():
+        h = jnp.int32(LAST)
+        for j in (1, 3, 2):
+            at_wait(h, same(j))
+        add_projected(h, [g, same(1), same(2), same(3)])
+        for j in (1, 3, 2):
+            at_wait(h, cross(j))
+        add_projected(h, [cross(j) for j in range(4)])
 
     far_row = {LEFT: 0, RIGHT: 1, FAR8: 2, LEFT2: 3, RIGHT2: 4}
 
@@ -311,7 +337,7 @@
             kv_start(h, 4, 6)
 
     def step(h, _):
-        @pl.when(h < HEADS_LOCAL - 2)
+        @pl.when(both(h < HEADS_LOCAL - 2, jnp.logical_or(h > 0, jnp.logical_not(middle))))
         def _():
             kv_start(h + 2, 1, 2, 0)
 
@@ -333,32 +359,28 @@
             kv_start(h + 1, 8)
             relay_near(h + 1)
 
+        @pl.when(both(h >= 2, h < DIRECT + 2))
+        def _():
+            relay_cross(h - 2)
+
         attend(h, LEFT)
         attend(h, RIGHT)
-
         kv_wait(h, FWD)
         attend(h, FWD)
 
         @pl.when(h >= 1)
         def _():
-            relay_attended(h - 1)
-
-        @pl.when(h == 2)
+            relay_partner(h - 1)
+
+        @pl.when(both(h >= 1, h < DIRECT + 1))
+        def _():
+            relay_same(h - 1)
+
+        @pl.when(h == LAST)
         def _():
             for i in range(7):
-                w_wait(i)
-                w_forward(i).start()
-
-        @pl.when(h == 3)
-        def _():
-            for i in range(7):
-                ws_wait(i)
-            project(0)
-            project(1)
-
-        @pl.when(h == 4)
-        def _():
-            project(2)
+                ws_wait(i, 1)
+                w_pass(i, 2).start()
 
         kv_wait(h, LEFT2)
         attend(h, LEFT2)
@@ -370,24 +392,43 @@
         at_copy(h, 1).start()
         at_copy(h, 2).start()
 
-        @pl.when(h == LAST)
+        @pl.when(h >= DIRECT)
         def _():
             at_copy(h, 7).start()
+
+        for after, blocks in enumerate(PASSED):
+            @pl.when(h == after)
+            def _(blocks=blocks):
+                for i in blocks:
+                    w_wait(i)
+                    w_pass(i, 0).start()
+                    w_pass(i, 1).start()
+
         return 0
 
     relay_far(0)
     kv_start(2, 3)
     relay_far(1)
     kv_start(3, 3)
+
+    @pl.when(middle)
+    def _():
+        kv_start(2, 1, 2, 0)
+
     relay_near(0)
     kv_wait(0, RELAY)
     kv_start(0, 8)
     relay_far(2)
     kv_start(4, 3)
     lax.fori_loop(0, HEADS_LOCAL, step, 0)
-    project(3)
-    relay_attended(LAST, last=True)
-    project(4)
+    relay_partner(LAST)
+    for i in range(7):
+        ws_wait(i, 0)
+        ws_wait(i, 2)
+    relay_cross(3)
+    for h in range(LAST):
+        project(h)
+    project_last()
     gate = gate_s[pl.ds(ts_ref[0], 1), :]
     out_ref[...] = (hid[...].astype(jnp.float32) + gate * proj[...]).astype(out_ref.dtype)
 
@@ -406,7 +447,8 @@
     lax.fori_loop(0, HEADS_LOCAL, drain, 0)
     for i in range(7):
         w_copy(i).wait_send()
-        w_forward(i).wait_send()
+        for kind in range(3):
+            w_pass(i, kind).wait_send()
 
 
 def body(hidden_in, queries, keys, values, radial_mask, out_weight, gate_table, timestep):
@@ -436,7 +478,7 @@
             dma((19,)),
             dma((9, HEADS_LOCAL)), dma((SLOTS, HEADS_LOCAL)),
             dma((7, HEADS_LOCAL)), dma((GROUPS, HEADS_LOCAL)),
-            dma((7,)), dma((GROUPS,)), dma((7,)), dma((GROUPS,)),
+            dma((7,)), dma((GROUPS,)), dma((3, 7)), dma((3, GROUPS)),
         ],
         compiler_params=pltpu.CompilerParams(
             collective_id=0, has_side_effects=True, vmem_limit_bytes=60 * 1024 * 1024),

time: 136 us -> 125 us (0.919)
  Pallas kernels: 133 us -> 122 us
    pallas_call x1, Pallas kernels: 133 us -> 122 us  [body(): pl.pallas_call(kernel, out_shape=jax.ShapeDtypeStruct((ROWS, ROWS), jnp.b...]
where the time goes in v3:
time: 125 us
  Pallas kernels  122 us (98%)
  local copies, waits for them, and re-layouts  2.11 us (2%)
    pallas_call x1, Pallas kernels, body(): pl.pallas_call(kernel, out_shape=jax.ShapeDtypeStruct((ROWS, ROWS), jnp.b...  122 us

profile of v3, /device:TPU:32, one launch (start us, length us, event | category | flops | bytes accessed | tf_op | source)
XLA Modules:
  0.0 124.7 jit_solution(18034377475938494265)
XLA Ops:
  0.7 121.9 %shard_map.82 = bf16[640,640]{1,0:T(8,128)(2,1)} custom-call(s32[1]{0:T(128)S(6)} %copy.10.ts_ref, s32[5,5,1,6]{3,2,1,0:T(1,128)} %bitcast.1, f32[50,640]{1,0:T(8,128)} %gate_hbm.1, bf16[640,640]{1,0:T(8,128)(2,1)} %hid_hbm.1, bf16[640,640]{1,0:T(8,128)(2,1)} %q_hbm.1, bf16[640,640]{1,0:T(8,128)(2,1)} %k_hbm.1, bf16[640,640]{1,0:T(8,128)(2,1)} %v_hbm.1, ...), custom_call_target="tpu_custom_call" | custom-call | flops 14000000000 | bytes 12000000 | tf_op jit(solution)/shard_map/pallas_call | solution.py:457
  122.6 2.1 %copy.11 = bf16[640,640]{1,0:T(8,128)(2,1)} copy(bf16[640,640]{1,0:T(8,128)(2,1)} %shard_map.82) | data formatting | bytes 1638400

commit v4 on v3

--- a/solution.py
+++ b/solution.py
@@ -17,8 +17,10 @@
 OWN, SIB, LEFT, RIGHT, FAR8, FWD, LEFT2, RIGHT2, RELAY = range(9)
 SCALE2 = 1.4426950408889634 * HEAD_DIM ** -0.5
 NEG = -1e30
+HALF = ROWS // 2
 QUARTER = ROWS // 4
-PASSED = ((0, 2), (1, 3), (4, 6), (5,))
+SHARED = (1, 5)
+PASSED = ((), (1, 5), (0, 2, 3), (4, 6))
 
 
 def both(*conds):
@@ -139,26 +141,31 @@
         RELAY: jnp.logical_or(is_a, is_d),
     }
 
+    def kv_wait_any(h, slot):
+        pltpu.make_async_remote_copy(
+            src_ref=kv.at[slot, h], dst_ref=kv.at[slot, h],
+            send_sem=kv_send.at[0, h], recv_sem=kv_recv.at[slot, h],
+            device_id=(sib, g), device_id_type=MESH).wait_recv()
+
     def kv_wait(h, slot):
         def wait():
-            pltpu.make_async_remote_copy(
-                src_ref=kv.at[slot, h], dst_ref=kv.at[slot, h],
-                send_sem=kv_send.at[0, h], recv_sem=kv_recv.at[slot, h],
-                device_id=(sib, g), device_id_type=MESH).wait_recv()
+            kv_wait_any(h, slot)
         if has[slot] is always:
             wait()
         else:
             pl.when(has[slot])(wait)
 
-    def quarter(on_core, on_zl):
-        return pl.ds(pl.multiple_of((on_core * 2 + on_zl) * QUARTER, 16), QUARTER)
+    def portion(i, on_core, on_zl):
+        if i in SHARED:
+            return pl.ds(pl.multiple_of((on_core * 2 + on_zl) * QUARTER, 16), QUARTER)
+        return pl.ds(pl.multiple_of(on_core * HALF, 16), HALF)
 
     w_peers = [(f, same(j), zl) for j in (1, 2, 3)] + [(f8, cross(j), 1 - zl) for j in range(4)]
 
     def w_copy(i):
         frame, group, their_zl = w_peers[i]
         cols = pl.ds(pl.multiple_of(group * ROWS, 128), ROWS)
-        rows = quarter(core, their_zl)
+        rows = portion(i, core, their_zl)
         return pltpu.make_async_remote_copy(
             src_ref=w_hbm.at[rows, cols], dst_ref=wcol.at[g, rows],
             send_sem=w_send.at[i], recv_sem=w_recv.at[g],
@@ -166,7 +173,7 @@
 
     def w_pass(i, kind):
         group = w_peers[i][1]
-        rows = quarter(core, zl if kind < 2 else 1 - zl)
+        rows = portion(i, core, zl if kind < 2 else 1 - zl)
         return pltpu.make_async_remote_copy(
             src_ref=wcol.at[group, rows], dst_ref=wcol.at[group, rows],
             send_sem=ws_send.at[kind, i], recv_sem=ws_recv.at[kind, group],
@@ -174,14 +181,14 @@
 
     def w_wait(i):
         group = w_peers[i][1]
-        ref = wcol.at[group, quarter(core, zl)]
+        ref = wcol.at[group, portion(i, core, zl)]
         pltpu.make_async_remote_copy(
             src_ref=ref, dst_ref=ref, send_sem=w_send.at[i], recv_sem=w_recv.at[group],
             device_id=(sib, g), device_id_type=MESH).wait_recv()
 
     def ws_wait(i, kind):
         group = w_peers[i][1]
-        ref = wcol.at[group, quarter(core if kind == 1 else 1 - core, zl if kind == 0 else 1 - zl)]
+        ref = wcol.at[group, portion(i, core if kind == 1 else 1 - core, zl if kind == 0 else 1 - zl)]
         pltpu.make_async_remote_copy(
             src_ref=ref, dst_ref=ref, send_sem=ws_send.at[kind, i], recv_sem=ws_recv.at[kind, group],
             device_id=(sib, g), device_id_type=MESH).wait_recv()
@@ -256,7 +263,11 @@
 
     far_row = {LEFT: 0, RIGHT: 1, FAR8: 2, LEFT2: 3, RIGHT2: 4}
 
-    def attend(h, slot):
+    def attend(h, slot, row=None, cond=None):
+        if cond is None:
+            row = far_row.get(slot)
+            cond = always if slot == OWN else has[slot]
+
         def run():
             s_all = lax.dot_general(
                 qs[h], kv[slot, h, 0], (((1,), (1,)), ((), ())),
@@ -265,8 +276,8 @@
             for b in range(ROWS // BLK):
                 rows = slice(b * BLK, (b + 1) * BLK)
                 s = s_all[rows]
-                if slot in far_row:
-                    s = s + bias[far_row[slot], b:b + 1, :]
+                if row is not None:
+                    s = s + bias[row, b:b + 1, :]
                 top = functools.reduce(
                     jnp.maximum, [s[:, i * 128:(i + 1) * 128] for i in range(5)])
                 old = m_s[rows, :]
@@ -280,7 +291,6 @@
             acc[...] += jnp.dot(
                 jnp.concatenate(weights, axis=0), kv[slot, h, 1],
                 preferred_element_type=jnp.float32)
-        cond = always if slot == OWN else has[slot]
         if cond is always:
             run()
         else:
@@ -365,27 +375,30 @@
 
         attend(h, LEFT)
         attend(h, RIGHT)
+
+        @pl.when(h >= 1)
+        def _():
+            relay_partner(h - 1)
+
+        @pl.when(both(h >= 1, h < DIRECT + 1))
+        def _():
+            relay_same(h - 1)
+
         kv_wait(h, FWD)
         attend(h, FWD)
 
-        @pl.when(h >= 1)
-        def _():
-            relay_partner(h - 1)
-
-        @pl.when(both(h >= 1, h < DIRECT + 1))
-        def _():
-            relay_same(h - 1)
-
         @pl.when(h == LAST)
         def _():
-            for i in range(7):
+            for i in SHARED:
                 ws_wait(i, 1)
                 w_pass(i, 2).start()
 
-        kv_wait(h, LEFT2)
-        attend(h, LEFT2)
-        kv_wait(h, RIGHT2)
-        attend(h, RIGHT2)
+        upper = f // 8
+        both_sides = both(f >= 4, f < 12)
+        pl.when(both_sides)(lambda: kv_wait_any(h, LEFT2 + upper))
+        attend(h, LEFT2 + upper, 3 + upper, both_sides)
+        kv_wait_any(h, RIGHT2 - upper)
+        attend(h, RIGHT2 - upper, 4 - upper, always)
         total = jnp.sum(l_s[...], axis=1, keepdims=True)
         att[g, h] = (acc[...] / total).astype(jnp.bfloat16)
         at_copy(h, 0).start()
@@ -402,7 +415,8 @@
                 for i in blocks:
                     w_wait(i)
                     w_pass(i, 0).start()
-                    w_pass(i, 1).start()
+                    if i in SHARED:
+                        w_pass(i, 1).start()
 
         return 0
 
@@ -424,7 +438,8 @@
     relay_partner(LAST)
     for i in range(7):
         ws_wait(i, 0)
-        ws_wait(i, 2)
+        if i in SHARED:
+            ws_wait(i, 2)
     relay_cross(3)
     for h in range(LAST):
         project(h)
@@ -447,7 +462,7 @@
     lax.fori_loop(0, HEADS_LOCAL, drain, 0)
     for i in range(7):
         w_copy(i).wait_send()
-        for kind in range(3):
+        for kind in range(3 if i in SHARED else 1):
             w_pass(i, kind).wait_send()
 
 

time: 125 us -> 124 us (level)
  no operation moved by 1% of the time
where the time goes in v4:
time: 124 us
  Pallas kernels  121 us (98%)
  local copies, waits for them, and re-layouts  2.11 us (2%)
    pallas_call x1, Pallas kernels, body(): pl.pallas_call(kernel, out_shape=jax.ShapeDtypeStruct((ROWS, ROWS), jnp.b...  121 us

profile of v4, /device:TPU:32, one launch (start us, length us, event | category | flops | bytes accessed | tf_op | source)
XLA Modules:
  0.0 123.6 jit_solution(6215342587012216363)
XLA Ops:
  0.7 120.8 %shard_map.82 = bf16[640,640]{1,0:T(8,128)(2,1)} custom-call(s32[1]{0:T(128)S(6)} %copy.10.ts_ref, s32[5,5,1,6]{3,2,1,0:T(1,128)} %bitcast.1, f32[50,640]{1,0:T(8,128)} %gate_hbm.1, bf16[640,640]{1,0:T(8,128)(2,1)} %hid_hbm.1, bf16[640,640]{1,0:T(8,128)(2,1)} %q_hbm.1, bf16[640,640]{1,0:T(8,128)(2,1)} %k_hbm.1, bf16[640,640]{1,0:T(8,128)(2,1)} %v_hbm.1, ...), custom_call_target="tpu_custom_call" | custom-call | flops 14000000000 | bytes 12000000 | tf_op jit(solution)/shard_map/pallas_call | solution.py:472
  121.5 2.1 %copy.11 = bf16[640,640]{1,0:T(8,128)(2,1)} copy(bf16[640,640]{1,0:T(8,128)(2,1)} %shard_map.82) | data formatting | bytes 1638400
